TPU v7x, 32 devices: a whole 2x2x4 slice. The times are simulated.
32 devices in a mesh: seq: 8 (over z, y), head: 4 (over x, core).
Axes of the slice: x: 2, y: 2, z: 4, core: 2. Of those that a mesh axis runs over, the one named last changes fastest.
Arguments:
- queries: bfloat16 [8192, 4096], P(('seq', 'head')), may hold values from -6 to 6
- key_rows: bfloat16 [8192, 4096], P(('seq', 'head')), may hold values from -6 to 6
- value_rows: bfloat16 [8192, 4096], P(('seq', 'head')), may hold values from -6 to 6
- decay_rates: float32 [32], replicated, as said below
- norm_gain: float32 [4096], replicated, may hold values from 0.5 to 1.5
Outputs:
- attended: bfloat16 [8192, 4096], P(('seq', 'head'))
Inputs may be any that keep to these rules, and one draw needn't show every extreme that they name: `decay_rates`: one positive rate per head.
All inputs are finite; a program needn't handle non-finite values.
Results may differ from a plain program's by a relative error of at most 0.003.
Values may be sent and summed in bfloat16 or wider, within the bound.
A program may use at most 512 MiB of HBM per device.

v0:
```python
import jax
import jax.numpy as jnp
from jax import lax
from jax.sharding import PartitionSpec as P

HEADS = 32
HEAD_DIM = 128
BLOCK = 256


def carried_in(shard, axis, combine, identity):
    size, here = (lax.axis_size(axis), lax.axis_index(axis))
    everything = jax.tree.map(lambda part: lax.all_gather(part, axis), shard)
    start = jax.tree.map(
        lambda part, zero: jnp.broadcast_to(jnp.asarray(zero, part.dtype), part.shape),
        shard,
        identity,
    )

    def hop(k, before):
        reached = k < here
        new = combine(before, jax.tree.map(lambda part: part[k], everything))
        return jax.tree.map(lambda a, b: jnp.where(reached, a, b), new, before)

    return lax.fori_loop(0, size, hop, start)


def block_chain(queries, key_rows, value_rows, rates, block):
    tokens, heads, width = queries.shape
    count = tokens // block
    q_blocks = queries.reshape(count, block, heads, width)
    k_blocks = key_rows.reshape(count, block, heads, width)
    v_blocks = value_rows.reshape(count, block, heads, width)
    positions = jnp.arange(block, dtype=jnp.float32)
    offsets = positions[:, None] - positions[None, :]
    within = jnp.where(
        offsets[None] >= 0.0, jnp.exp(-rates[:, None, None] * jnp.maximum(offsets, 0.0)[None]), 0.0
    )
    q_decay = jnp.exp(-rates[None, :] * (positions[:, None] + 1.0))[:, :, None]
    k_decay = jnp.exp(-rates[None, :] * (block - 1.0 - positions[:, None]))[:, :, None]
    carry_decay = jnp.exp(-rates * block)[:, None, None]

    def advance(state, items):
        q_part, k_part, v_part = items
        scores = jnp.einsum("ihe,jhe->hij", q_part, k_part, preferred_element_type=jnp.float32)
        weights = (scores * within).astype(jnp.bfloat16)
        intra = jnp.einsum("hij,jhe->ihe", weights, v_part, preferred_element_type=jnp.float32)
        inter = jnp.einsum(
            "ihe,hef->ihf",
            q_part.astype(jnp.float32) * q_decay,
            state,
            precision=lax.Precision.HIGHEST,
        )
        added = jnp.einsum(
            "jhe,jhf->hef",
            k_part.astype(jnp.float32) * k_decay,
            v_part.astype(jnp.float32),
            precision=lax.Precision.HIGHEST,
        )
        return (carry_decay * state + added, intra + inter)

    start = jnp.zeros((heads, width, width), jnp.float32)
    state, outputs = lax.scan(advance, start, (q_blocks, k_blocks, v_blocks))
    return (outputs.reshape(tokens, heads, width), state)


def combine_states(earlier, later):
    return (earlier[0] * later[0], later[0][:, None, None] * earlier[1] + later[1])


def add_incoming(partial_value, queries, rates, incoming):
    span = queries.shape[0]
    positions = jnp.arange(span, dtype=jnp.float32)
    q_decay = jnp.exp(-rates[None, :] * (positions[:, None] + 1.0))[:, :, None]
    return partial_value + jnp.einsum(
        "ihe,hef->ihf",
        queries.astype(jnp.float32) * q_decay,
        incoming,
        precision=lax.Precision.HIGHEST,
    )


def normalize(total, gains):
    mean_square = jnp.mean(total * total, axis=-1, keepdims=True)
    normed = (total * lax.rsqrt(mean_square + 1e-06) * gains).astype(jnp.bfloat16)
    return normed.reshape(total.shape[0], total.shape[1] * total.shape[2])


def body(queries, key_rows, value_rows, decay_rates, norm_gain):
    group_heads = HEADS // lax.axis_size("head")
    first_head = lax.axis_index("head") * group_heads
    rates = lax.dynamic_slice_in_dim(decay_rates, first_head, group_heads)
    gains = lax.dynamic_slice_in_dim(
        norm_gain, first_head * HEAD_DIM, group_heads * HEAD_DIM
    ).reshape(group_heads, HEAD_DIM)
    q_group, k_group, v_group = (
        lax.all_to_all(queries, "head", split_axis=1, concat_axis=0, tiled=True),
        lax.all_to_all(key_rows, "head", split_axis=1, concat_axis=0, tiled=True),
        lax.all_to_all(value_rows, "head", split_axis=1, concat_axis=0, tiled=True),
    )
    span = q_group.shape[0]
    shaped = (span, group_heads, HEAD_DIM)
    q_group = q_group.reshape(shaped)
    partial_value, local_state = block_chain(
        q_group, k_group.reshape(shaped), v_group.reshape(shaped), rates, BLOCK
    )
    span_decay = jnp.exp(-rates * span)
    identity = (jnp.ones_like(span_decay), jnp.zeros_like(local_state))
    _, incoming = carried_in((span_decay, local_state), "seq", combine_states, identity)
    total = add_incoming(partial_value, q_group, rates, incoming)
    normed = normalize(total, gains)
    return lax.all_to_all(normed, "head", split_axis=0, concat_axis=1, tiled=True)


def solution(mesh):
    return jax.shard_map(
        body,
        mesh=mesh,
        in_specs=(
            P(("seq", "head"), None),
            P(("seq", "head"), None),
            P(("seq", "head"), None),
            P(),
            P(),
        ),
        out_specs=P(("seq", "head"), None),
        check_vma=False,
    )
```

profile of v0, /device:TPU:1, one launch (start us, length us, event | category | flops | bytes accessed | tf_op | source)
XLA Modules:
  0.0 368.5 jit_solution(18076343051067585176)
XLA Ops:
  6.5 4.1 %copy.55 = bf16[256,4096]{0,1:T(8,128)(2,1)} copy(bf16[256,4096]{1,0:T(8,128)(2,1)} %param.10) | data formatting | bytes 4194304 | tf_op args[1]
  10.6 4.6 %all-to-all-start = ((bf16[256,4,1024]{0,2,1:T(8,128)(2,1)}), bf16[256,4,1024]{0,2,1:T(8,128)(2,1)}, u32[]{:S(2)}, u32[]{:S(2)}) async-start(bf16[256,4,1024]{0,2,1:T(8,128)(2,1)} %bitcast.1), calls=%async_computation | async-start | bytes 4194304 | tf_op jit(solution)/shard_map/all_to_all | solution.py:98
  17.7 22.7 %all-to-all-done = bf16[256,4,1024]{0,2,1:T(8,128)(2,1)} async-done(((bf16[256,4,1024]{0,2,1:T(8,128)(2,1)}), bf16[256,4,1024]{0,2,1:T(8,128)(2,1)}, u32[]{:S(2)}, u32[]{:S(2)}) %all-to-all-start) | async-done | bytes 2097184 | tf_op jit(solution)/shard_map/all_to_all | solution.py:98
  40.4 5.8 %all-to-all-start.1 = ((bf16[256,4,1024]{0,2,1:T(8,128)(2,1)}), bf16[256,4,1024]{0,2,1:T(8,128)(2,1)}, u32[]{:S(2)}, u32[]{:S(2)}) async-start(bf16[256,4,1024]{0,2,1:T(8,128)(2,1)} %bitcast.4), calls=%async_computation.1 | async-start | bytes 4194304 | tf_op jit(solution)/shard_map/all_to_all | solution.py:99
  48.6 22.5 %all-to-all-done.1 = bf16[256,4,1024]{0,2,1:T(8,128)(2,1)} async-done(((bf16[256,4,1024]{0,2,1:T(8,128)(2,1)}), bf16[256,4,1024]{0,2,1:T(8,128)(2,1)}, u32[]{:S(2)}, u32[]{:S(2)}) %all-to-all-start.1) | async-done | bytes 2097184 | tf_op jit(solution)/shard_map/all_to_all | solution.py:99
  71.2 5.4 %all-to-all-start.2 = ((bf16[256,4,1024]{0,2,1:T(8,128)(2,1)}), bf16[256,4,1024]{0,2,1:T(8,128)(2,1)}, u32[]{:S(2)}, u32[]{:S(2)}) async-start(bf16[256,4,1024]{0,2,1:T(8,128)(2,1)} %bitcast.7), calls=%async_computation.2 | async-start | bytes 4194304 | tf_op jit(solution)/shard_map/all_to_all | solution.py:97
  78.2 23.3 %all-to-all-done.2 = bf16[256,4,1024]{0,2,1:T(8,128)(2,1)} async-done(((bf16[256,4,1024]{0,2,1:T(8,128)(2,1)}), bf16[256,4,1024]{0,2,1:T(8,128)(2,1)}, u32[]{:S(2)}, u32[]{:S(2)}) %all-to-all-start.2) | async-done | bytes 2097184 | tf_op jit(solution)/shard_map/all_to_all | solution.py:97
  101.5 130.3 %while.30 = (s32[]{:T(128)}, f32[8,128,128]{2,1,0:T(8,128)S(1)}, f32[4,256,8,128]{1,0,3,2:T(4,128)}, f32[8,1,1]{0,2,1:T(1,128)S(1)}, bf16[4,256,8,128]{1,3,2,0:T...) while((s32[]{:T(128)}, f32[8,128,128]{2,1,0:T(8,128)S(1)}, ...), condition=%wide.region_1.2_spmd.clone.clone.clone, body=%wide.region_0.1_spmd.clone.clone.clone.sunk | while | flops 1077678080 | bytes 16617220 | solution.py:63
  110.7 23.4 %dynamic_update_slice.8 = f32[4,256,8,128]{1,0,3,2:T(4,128)} dynamic-update-slice(f32[4,256,8,128]{1,0,3,2:T(4,128)} %get-tuple-element.510, f32[1,256,8,128]{1,0,3,2:T(1,128)S(1)} %copy.90, s32[]{:T(128)S(6)} %copy.96, s32[]{:T(128)} %constant.58.clone.1..sunk.1, s32[]{:T(128)} %constant.58.clone.1..sunk.1, s32[]{:T(128)} %constant.58.clone.1..sunk.1) | dynamic-update-slice | bytes 2097156 | tf_op jit(solution)/shard_map/while/body/jit(dynamic_update_index_in_dim)/dynamic_update_slice | solution.py:63
  143.3 23.4 %dynamic_update_slice.8 = f32[4,256,8,128]{1,0,3,2:T(4,128)} dynamic-update-slice(f32[4,256,8,128]{1,0,3,2:T(4,128)} %get-tuple-element.510, f32[1,256,8,128]{1,0,3,2:T(1,128)S(1)} %copy.90, s32[]{:T(128)S(6)} %copy.96, s32[]{:T(128)} %constant.58.clone.1..sunk.1, s32[]{:T(128)} %constant.58.clone.1..sunk.1, s32[]{:T(128)} %constant.58.clone.1..sunk.1) | dynamic-update-slice | bytes 2097156 | tf_op jit(solution)/shard_map/while/body/jit(dynamic_update_index_in_dim)/dynamic_update_slice | solution.py:63
  175.8 23.4 %dynamic_update_slice.8 = f32[4,256,8,128]{1,0,3,2:T(4,128)} dynamic-update-slice(f32[4,256,8,128]{1,0,3,2:T(4,128)} %get-tuple-element.510, f32[1,256,8,128]{1,0,3,2:T(1,128)S(1)} %copy.90, s32[]{:T(128)S(6)} %copy.96, s32[]{:T(128)} %constant.58.clone.1..sunk.1, s32[]{:T(128)} %constant.58.clone.1..sunk.1, s32[]{:T(128)} %constant.58.clone.1..sunk.1) | dynamic-update-slice | bytes 2097156 | tf_op jit(solution)/shard_map/while/body/jit(dynamic_update_index_in_dim)/dynamic_update_slice | solution.py:63
  208.4 23.4 %dynamic_update_slice.8 = f32[4,256,8,128]{1,0,3,2:T(4,128)} dynamic-update-slice(f32[4,256,8,128]{1,0,3,2:T(4,128)} %get-tuple-element.510, f32[1,256,8,128]{1,0,3,2:T(1,128)S(1)} %copy.90, s32[]{:T(128)S(6)} %copy.96, s32[]{:T(128)} %constant.58.clone.1..sunk.1, s32[]{:T(128)} %constant.58.clone.1..sunk.1, s32[]{:T(128)} %constant.58.clone.1..sunk.1) | dynamic-update-slice | bytes 2097156 | tf_op jit(solution)/shard_map/while/body/jit(dynamic_update_index_in_dim)/dynamic_update_slice | solution.py:63
  232.7 19.3 %all-reduce = f32[64]{0:T(128)S(1)} all-reduce(f32[64]{0:T(128)S(1)} %get-tuple-element.372), channel_id=2, replica_groups=mesh['seq'=8,'head'=4] {'seq'}, use_global_device_ids=true, to_apply=%add | all-reduce | flops 64 | bytes 512
  252.4 5.8 %reshape.189 = f32[1024,8,128]{0,2,1:T(8,128)} reshape(f32[4,256,8,128]{1,0,3,2:T(4,128)} %get-tuple-element.152) | data formatting | bytes 8388608 | tf_op jit(solution)/shard_map/reshape | solution.py:64
  258.2 3.9 %bitcast_convert_fusion = f32[4,256,1024]{1,2,0:T(8,128)} fusion(bf16[256,4,1024]{0,2,1:T(8,128)(2,1)} %all-to-all-done.2), kind=kLoop, calls=%fused_computation.49 | loop fusion | flops 1048576 | bytes 6291456 | tf_op jit(solution)/shard_map/convert_element_type | solution.py:77
  262.1 5.4 %copy.62 = f32[4,256,1024]{2,1,0:T(8,128)} copy(f32[4,256,1024]{1,2,0:T(8,128)} %bitcast_convert_fusion) | data formatting | bytes 8388608 | tf_op jit(solution)/shard_map/convert_element_type | solution.py:77
  267.5 3.7 %copy.78 = f32[128,8,8,128]{3,2,1,0:T(8,128)S(1)} copy(f32[128,8,8,128]{3,1,2,0:T(8,128)} %bitcast.105) | data formatting | bytes 8388608
  271.2 3.9 %bitcast_multiply_fusion = f32[1024,8,128]{2,1,0:T(8,128)} fusion(f32[128,8,8,128]{3,2,1,0:T(8,128)S(1)} %copy.78, f32[1024,8]{1,0:T(8,128)S(1)} %copy.63), kind=kLoop, calls=%fused_computation.43 | loop fusion | flops 1048576 | bytes 8421376 | tf_op jit(solution)/shard_map/mul | solution.py:77
  275.1 31.4 %all-gather.4.cloned.1.call-done = f32[64,128,128]{2,1,0:T(8,128)} async-done(((f32[8,128,128]{2,1,0:T(8,128)}), f32[64,128,128]{2,1,0:T(8,128)}) %all-gather.4.cloned.1.call-update) | async-done | bytes 4194320 | tf_op jit(solution)/shard_map/all_gather | solution.py:13
  306.5 9.7 %while.29 = (s32[]{:T(128)}, f32[8,128,128]{2,1,0:T(8,128)S(1)}, s32[]{:T(128)}, f32[8,8]{1,0:T(8,128)S(1)}, f32[8,8,128,128]{3,2,1,0:T(8,128)}, /*index=5*/s32[]{:T(128)}, s32[]{:T(128)}) while((s32[]{:T(128)}, f32[8,128,128]{2,1,0:T(8,128)S(1)}, s32[]{:T(128)}, f32[8,8]{1,0:T(8,128)S(1)}, f32[8,8,128,128]{3,2,1,0:T(8,128)}, ...), condition=%wide.region_3.4_spmd.clone, body=%wide.region_2.3_spmd.clone.sunk | while | flops 524292 | bytes 1573073 | solution.py:25
  316.2 8.1 %multiply_reduce_fusion = (f32[1024,8]{0,1:T(8,128)S(1)}, f32[1024,8,128]{0,2,1:T(8,128)S(1)}) fusion(f32[1024,8,128]{0,2,1:T(8,128)} %reshape.189, f32[8,128,128]{2,1,0:T(8,128)S(1)} %get-tuple-element.154, f32[1024,8,128]{2,1,0:T(8,128)} %bitcast_multiply_fusion), kind=kOutput, calls=%fused_computation.48 | convolution fusion | flops 1613750272 | bytes 13139968 | tf_op jit(solution)/shard_map/ihe,hef->ihf/dot_general | solution.py:75
  326.1 3.3 all_to_all.59
  329.7 29.1 %all_to_all.67 = bf16[4,256,1024]{1,2,0:T(8,128)(2,1)S(1)} all-to-all(bf16[4,256,1024]{1,2,0:T(8,128)(2,1)S(1)} %copy.66), channel_id=1, replica_groups=mesh['seq'=8,'head'=4] {'head'}, dimensions={0} | all-to-all | bytes 4194304 | tf_op jit(solution)/shard_map/all_to_all | solution.py:112
  358.8 2.8 copy.67
  (84 shorter events, 55.0 us)
Async XLA Ops:
  6.5 245.8 %copy-start = (f32[4096]{0:T(1024)S(1)}, f32[4096]{0:T(1024)}, u32[]{:S(2)}) copy-start(f32[4096]{0:T(1024)} %param.13) | copy-start | bytes 49156
  10.6 4.6 %copy-start.3 = (bf16[256,4096]{1,0:T(8,128)(2,1)S(1)}, bf16[256,4096]{1,0:T(8,128)(2,1)}, u32[]{:S(2)}) copy-start(bf16[256,4096]{1,0:T(8,128)(2,1)} %param.11) | copy-start | bytes 6291460
  10.6 29.8 %all-to-all-start = ((bf16[256,4,1024]{0,2,1:T(8,128)(2,1)}), bf16[256,4,1024]{0,2,1:T(8,128)(2,1)}, u32[]{:S(2)}, u32[]{:S(2)}) async-start(bf16[256,4,1024]{0,2,1:T(8,128)(2,1)} %bitcast.1), calls=%async_computation | async-start | bytes 4194304 | tf_op jit(solution)/shard_map/all_to_all | solution.py:98
  40.4 5.8 %copy-start.4 = (bf16[256,4096]{1,0:T(8,128)(2,1)S(1)}, bf16[256,4096]{1,0:T(8,128)(2,1)}, u32[]{:S(2)}) copy-start(bf16[256,4096]{1,0:T(8,128)(2,1)} %param.9) | copy-start | bytes 6291460
  40.4 30.7 %all-to-all-start.1 = ((bf16[256,4,1024]{0,2,1:T(8,128)(2,1)}), bf16[256,4,1024]{0,2,1:T(8,128)(2,1)}, u32[]{:S(2)}, u32[]{:S(2)}) async-start(bf16[256,4,1024]{0,2,1:T(8,128)(2,1)} %bitcast.4), calls=%async_computation.1 | async-start | bytes 4194304 | tf_op jit(solution)/shard_map/all_to_all | solution.py:99
  71.1 5.5 %copy-start.6 = (u32[32]{0:T(128)S(1)}, u32[32]{0:T(128)}, u32[]{:S(2)}) copy-start(u32[32]{0:T(128)} %constant.75) | copy-start | bytes 388
  71.1 6.7 %copy-start.5 = (f32[32]{0:T(128)S(1)}, f32[32]{0:T(128)}, u32[]{:S(2)}) copy-start(f32[32]{0:T(128)} %param.12) | copy-start | bytes 388
  71.2 30.4 %all-to-all-start.2 = ((bf16[256,4,1024]{0,2,1:T(8,128)(2,1)}), bf16[256,4,1024]{0,2,1:T(8,128)(2,1)}, u32[]{:S(2)}, u32[]{:S(2)}) async-start(bf16[256,4,1024]{0,2,1:T(8,128)(2,1)} %bitcast.7), calls=%async_computation.2 | async-start | bytes 4194304 | tf_op jit(solution)/shard_map/all_to_all | solution.py:97
  76.6 229.9 %all-gather.4.cloned.1.call-start = ((), (), s32[]{:S(2)}) async-start(), calls=%async_computation.4 | async-start | bytes 4718592 | tf_op jit(solution)/shard_map/all_gather | solution.py:13
  231.8 0.8 copy-start.2
  358.8 2.9 copy-start.1
Sparse Core Ops, SparseCore 0:
  232.8 73.6 all-gather.3
where the time goes:
time: 373 us; the launch traced here: 368 us
  local copies, waits for them, and re-layouts  137 us (37%)
  waiting for transfers between devices  99.9 us (27%)
  blocking collectives  48.4 us (13%)
  matrix products  32.6 us (9%)
  other arithmetic  19.7 us (5%)
  starting transfers between devices  15.8 us (4%)
  between operations  14.2 us (4%)
    dynamic_update_slice x8, local copies, waits for them, and re-layouts, block_chain(): state, outputs = lax.scan(advance, start, (q_blocks, k_blocks, v_blocks))  98 us
    all_gather x1, waiting for transfers between devices, carried_in(): everything = jax.tree.map(lambda part: lax.all_gather(part, axis), shard)  31.4 us
    all_to_all x1, blocking collectives, body(): lax.all_to_all(normed, 'head', split_axis=0, concat_axis=1, tiled=True)  29.1 us
    all_to_all x1, waiting for transfers between devices, body(): lax.all_to_all(queries, 'head', split_axis=1, concat_axis=0, tiled=True)  23.3 us
    all_to_all x1, waiting for transfers between devices, body(): lax.all_to_all(key_rows, 'head', split_axis=1, concat_axis=0, tiled=True)  22.7 us
    all_to_all x1, waiting for transfers between devices, body(): lax.all_to_all(value_rows, 'head', split_axis=1, concat_axis=0, tiled=True)  22.5 us
    unnamed x1, blocking collectives  19.3 us
    unnamed x20, local copies, waits for them, and re-layouts  14.1 us
  transfers between devices with their start and end apart: 4, of which 4 were waited for; matrix products, arithmetic and copies ran while one was open for 8% of the time, Pallas kernels for 0%

commit v1 on v0

v1 whole, which is shorter than its diff:
```python
import functools
import jax
import jax.numpy as jnp
from jax import lax
from jax.experimental import pallas as pl
from jax.experimental.pallas import tpu as pltpu
from jax.sharding import PartitionSpec as P

HEADS = 32
HEAD_DIM = 128
BLOCK = 256
CHUNKS = 4
PER_SLOT = 4
F32 = jnp.float32
BF16 = jnp.bfloat16


def split_two(x):
    high = x.astype(BF16)
    low = (x - high.astype(F32)).astype(BF16)
    return jnp.concatenate([high, low], axis=1)


def kernel(
    levels, minor, q_hbm, k_hbm, v_hbm, rates, gains, out_hbm,
    q_ref, k_ref, v_ref, o_ref, total, aggs, lefts, ups, states, downs,
    in_sem, out_sem, up_send, up_recv, dn_send, dn_recv,
):
    heads = HEADS // CHUNKS
    rows = heads * HEAD_DIM
    width = heads * HEAD_DIM
    here = lax.axis_index("seq") * minor + lax.axis_index("head")
    bits = [(here // (1 << k)) % 2 for k in range(levels)]
    partners = []
    for k in range(levels):
        other = here + (1 - 2 * bits[k]) * (1 << k)
        partners.append((other // minor, other % minor))
    starts = [0]
    for k in range(levels - 1):
        starts.append(starts[k] + bits[k] * (rows >> (k + 1)))

    barrier = pltpu.get_barrier_semaphore()
    for partner in partners:
        pl.semaphore_signal(barrier, inc=1, device_id=partner, device_id_type=pl.DeviceIdType.MESH)

    def load(i, c):
        cols = pl.ds(c * width, width)
        src, dst = ((k_hbm, k_ref), (v_hbm, v_ref), (q_hbm, q_ref))[i]
        return pltpu.make_async_copy(src.at[:, cols], dst.at[:, cols], in_sem.at[i, c])

    def save(c):
        cols = pl.ds(c * width, width)
        return pltpu.make_async_copy(o_ref.at[:, cols], out_hbm.at[:, cols], out_sem.at[c])

    for c in range(CHUNKS):
        load(0, c).start()
        load(1, c).start()
    for c in range(CHUNKS):
        load(2, c).start()

    def up_copy(k, c):
        half = rows >> (k + 1)
        if k == levels - 1:
            src = aggs[k].at[c]
        else:
            src = aggs[k].at[c, pl.ds(pl.multiple_of((1 - bits[k]) * half, 8), half)]
        return pltpu.make_async_remote_copy(
            src_ref=src, dst_ref=ups[k].at[c],
            send_sem=up_send.at[k, c], recv_sem=up_recv.at[k, c],
            device_id=partners[k], device_id_type=pl.DeviceIdType.MESH,
        )

    def down_copy(k, c):
        half = rows >> (k + 1)
        spot = pl.ds(pl.multiple_of(bits[k] * half, 8), half)
        return pltpu.make_async_remote_copy(
            src_ref=downs[k].at[c], dst_ref=states[k].at[c, spot],
            send_sem=dn_send.at[k, c], recv_sem=dn_recv.at[k, c],
            device_id=partners[k], device_id_type=pl.DeviceIdType.MESH,
        )

    def head_cols(h):
        return pl.ds(pl.multiple_of(h * HEAD_DIM, HEAD_DIM), HEAD_DIM)

    positions = lax.broadcasted_iota(jnp.int32, (BLOCK, HEAD_DIM), 0).astype(F32)

    def local_states(c):
        def one(i, _):
            h = c * heads + i
            cols = head_cols(h)
            decay = jnp.exp(-rates[h] * (BLOCK - 1.0 - positions))
            wide = split_two(v_ref[:, cols].astype(F32) * decay)
            both = lax.dot_general(
                k_ref[:, cols], wide, (((0,), (0,)), ((), ())), preferred_element_type=F32
            )
            aggs[0][c, pl.ds(pl.multiple_of(i * HEAD_DIM, HEAD_DIM), HEAD_DIM), :] = (
                both[:, :HEAD_DIM] + both[:, HEAD_DIM:]
            )
            return 0

        lax.fori_loop(0, heads, one, 0, unroll=2)

    def segments(k, c):
        half = rows >> (k + 1)
        size = min(half, HEAD_DIM)
        for i in range(half // size):
            head = c * heads + (starts[k + 1] + i * size) // HEAD_DIM
            span = float(BLOCK << k)
            decay = jnp.exp(jnp.full((1, HEAD_DIM), -rates[head] * span, F32))
            yield i * size, size, decay

    def merge_up(k, c):
        half = rows >> (k + 1)
        left = bits[k] == 0
        for at, size, decay in segments(k, c):
            own = aggs[k][c, pl.ds(pl.multiple_of(bits[k] * half + at, 8), size), :]
            got = ups[k][c, pl.ds(at, size), :]
            first = jnp.where(left, own, got)
            second = jnp.where(left, got, own)
            lefts[k][c, pl.ds(at, size), :] = first
            aggs[k + 1][c, pl.ds(at, size), :] = decay * first + second

    def split_down(k, c):
        half = rows >> (k + 1)
        left = bits[k] == 0
        for at, size, decay in segments(k, c):
            before = states[k + 1][c, pl.ds(at, size), :]
            after = decay * before + lefts[k][c, pl.ds(at, size), :]
            states[k][c, pl.ds(pl.multiple_of(bits[k] * half + at, 8), size), :] = jnp.where(
                left, before, after
            )
            downs[k][c, pl.ds(at, size), :] = jnp.where(left, after, before)

    distance = (
        lax.broadcasted_iota(jnp.int32, (BLOCK, BLOCK), 0)
        - lax.broadcasted_iota(jnp.int32, (BLOCK, BLOCK), 1)
    )

    def inside(first, count):
        def one(i, _):
            h = first + i
            cols = head_cols(h)
            scores = lax.dot_general(
                q_ref[:, cols], k_ref[:, cols], (((1,), (1,)), ((), ())), preferred_element_type=F32
            )
            steps = jnp.maximum(distance, 0).astype(F32)
            within = jnp.where(distance >= 0, jnp.exp(-rates[h] * steps), 0.0)
            weights = (scores * within).astype(BF16)
            total[:, cols] = jnp.dot(weights, v_ref[:, cols], preferred_element_type=F32)
            return 0

        lax.fori_loop(0, count, one, 0, unroll=2)

    def finish(c):
        def one(i, _):
            h = c * heads + i
            cols = head_cols(h)
            state = states[0][c, pl.ds(pl.multiple_of(i * HEAD_DIM, HEAD_DIM), HEAD_DIM), :]
            both = jnp.dot(q_ref[:, cols], split_two(state), preferred_element_type=F32)
            inter = both[:, :HEAD_DIM] + both[:, HEAD_DIM:]
            decay = jnp.exp(-rates[h] * (positions + 1.0))
            value = total[:, cols] + decay * inter
            mean_square = jnp.mean(value * value, axis=-1, keepdims=True)
            normed = value * lax.rsqrt(mean_square + 1e-06) * gains[:, cols]
            o_ref[:, cols] = normed.astype(BF16)
            return 0

        lax.fori_loop(0, heads, one, 0, unroll=2)

    top = levels - 1

    def event(e, c):
        if e == 0:
            load(0, c).wait()
            load(1, c).wait()
            local_states(c)
            if c == 0:
                pl.semaphore_wait(barrier, levels)
            up_copy(0, c).start()
        elif e <= top:
            up_copy(e - 1, c).wait_recv()
            merge_up(e - 1, c)
            up_copy(e, c).start()
        else:
            k = 2 * top - e
            if k == top - 1:
                up_copy(top, c).wait_recv()
                got = ups[top][c]
                states[top][c] = jnp.where(bits[top] == 1, got, jnp.zeros_like(got))
            else:
                down_copy(k + 1, c).wait_recv()
            if k >= 0:
                split_down(k, c)
                down_copy(k, c).start()
            else:
                finish(c)
                save(c).start()

    last = 2 * top + 1
    done = 0
    for slot in range(last + CHUNKS):
        for c in range(CHUNKS):
            if 0 <= slot - c <= last:
                if slot - c == last:
                    while done < (c + 1) * heads:
                        inside(done, PER_SLOT)
                        done += PER_SLOT
                event(slot - c, c)
        if slot >= 1 and done < HEADS:
            if done % heads == 0:
                load(2, done // heads).wait()
            inside(done, PER_SLOT)
            done += PER_SLOT
    for c in range(CHUNKS):
        for k in range(levels):
            up_copy(k, c).wait_send()
        for k in range(top):
            down_copy(k, c).wait_send()
        save(c).wait()


def body(queries, key_rows, value_rows, decay_rates, norm_gain):
    major, minor = lax.axis_size("seq"), lax.axis_size("head")
    levels = (major * minor).bit_length() - 1
    assert major * minor == 1 << levels and queries.shape[0] == BLOCK
    rows = HEADS // CHUNKS * HEAD_DIM

    def pieces(first, count):
        return [pltpu.VMEM((CHUNKS, rows >> k, HEAD_DIM), F32) for k in range(first, first + count)]

    top = levels - 1
    full = (BLOCK, HEADS * HEAD_DIM)
    anywhere = pl.BlockSpec(memory_space=pl.ANY)
    return pl.pallas_call(
        functools.partial(kernel, levels, minor),
        out_shape=jax.ShapeDtypeStruct(full, BF16),
        in_specs=[
            anywhere, anywhere, anywhere,
            pl.BlockSpec(memory_space=pltpu.SMEM),
            pl.BlockSpec(memory_space=pltpu.VMEM),
        ],
        out_specs=anywhere,
        scratch_shapes=[
            pltpu.VMEM(full, BF16), pltpu.VMEM(full, BF16), pltpu.VMEM(full, BF16),
            pltpu.VMEM(full, BF16), pltpu.VMEM(full, F32),
            pieces(0, levels),
            pieces(1, top),
            pieces(1, top) + pieces(top, 1),
            pieces(0, levels),
            pieces(1, top),
            pltpu.SemaphoreType.DMA((3, CHUNKS)),
            pltpu.SemaphoreType.DMA((CHUNKS,)),
            pltpu.SemaphoreType.DMA((levels, CHUNKS)),
            pltpu.SemaphoreType.DMA((levels, CHUNKS)),
            pltpu.SemaphoreType.DMA((top, CHUNKS)),
            pltpu.SemaphoreType.DMA((top, CHUNKS)),
        ],
        compiler_params=pltpu.CompilerParams(
            collective_id=0, has_side_effects=True, vmem_limit_bytes=48 << 20
        ),
        cost_estimate=pl.CostEstimate(flops=2 << 30, bytes_accessed=8 << 20, transcendentals=4 << 20),
    )(queries, key_rows, value_rows, decay_rates, norm_gain.reshape(1, HEADS * HEAD_DIM))


def solution(mesh):
    tokens = P(("seq", "head"), None)
    return jax.shard_map(
        body,
        mesh=mesh,
        in_specs=(tokens, tokens, tokens, P(), P()),
        out_specs=tokens,
        check_vma=False,
    )
```

time: 373 us -> 54.9 us (0.15); the launches traced: 368 us -> 54.7 us
  local copies, waits for them, and re-layouts: 137 us -> 4.28 us
  waiting for transfers between devices: 99.9 us -> 0 us
  Pallas kernels: 0 us -> 50.4 us
  blocking collectives: 48.4 us -> 0 us
  matrix products: 32.6 us -> 0 us
  other arithmetic: 19.7 us -> 0 us
  starting transfers between devices: 15.8 us -> 0 us
  between operations: 14.2 us -> 0.01 us
    dynamic_update_slice x8 -> x0, local copies, waits for them, and re-layouts: 98 us -> none  [block_chain(): state, outputs = lax.scan(advance, start, (q_blocks, k_blocks, v_blocks))]
    all_to_all x3 -> x0, waiting for transfers between devices: 68.5 us -> none  [the longest x1 23.3 us: body(): lax.all_to_all(queries, 'head', split_axis=1, concat_axis=0, tiled=True)]
    pallas_call x0 -> x1, Pallas kernels: none -> 50.4 us  [body(): pl.pallas_call(functools.partial(kernel, levels, minor), out_shape=jax.Sh...]
    dot_general x13 -> x0, matrix products: 32.6 us -> none  [the longest x4 9.67 us: advance(): jnp.einsum('jhe,jhf->hef', k_part.astype(jnp.float32) * k_decay, v_part.a...]
    all_gather x1 -> x0, waiting for transfers between devices: 31.4 us -> none  [carried_in(): everything = jax.tree.map(lambda part: lax.all_gather(part, axis), shard)]
    all_to_all x1 -> x0, blocking collectives: 29.1 us -> none  [body(): lax.all_to_all(normed, 'head', split_axis=0, concat_axis=1, tiled=True)]
    unnamed x1 -> x0, blocking collectives: 19.3 us -> none
    all_to_all x3 -> x0, starting transfers between devices: 15.8 us -> none  [the longest x1 5.79 us: body(): lax.all_to_all(value_rows, 'head', split_axis=1, concat_axis=0, tiled=True)]
  transfers between devices with their start and end apart: 4 -> 0, of which waited for: 4 -> 0; matrix products, arithmetic and copies ran while one was open for 8% -> 0% of each run, Pallas kernels for 0% -> 0%
where the time goes in v1:
time: 54.9 us; the launch traced here: 54.7 us
  Pallas kernels  50.4 us (92%)
  local copies, waits for them, and re-layouts  4.28 us (8%)
    pallas_call x1, Pallas kernels, body(): pl.pallas_call(functools.partial(kernel, levels, minor), out_shape=jax.Sh...  50.4 us
    unnamed x7, local copies, waits for them, and re-layouts  4.28 us

profile of v1, /device:TPU:1, one launch (start us, length us, event | category | flops | bytes accessed | tf_op | source)
XLA Modules:
  0.0 54.7 jit_solution(14872148673908249207)
XLA Ops:
  0.0 0.0 copy-start
  0.0 1.6 %copy-done = bf16[256,4096]{1,0:T(8,128)(2,1)S(1)} copy-done((bf16[256,4096]{1,0:T(8,128)(2,1)S(1)}, bf16[256,4096]{1,0:T(8,128)(2,1)}, u32[]{:S(2)}) %copy-start) | copy-done | bytes 2097176
  1.6 0.0 copy-start.1
  1.6 0.7 %copy-done.1 = f32[4096]{0:T(1024)S(1)} copy-done((f32[4096]{0:T(1024)S(1)}, f32[4096]{0:T(1024)}, u32[]{:S(2)}) %copy-start.1) | copy-done | bytes 16408
  2.3 0.0 copy-start.2
  2.3 0.7 %copy-done.2 = f32[32]{0:T(128)S(1)} copy-done((f32[32]{0:T(128)S(1)}, f32[32]{0:T(128)}, u32[]{:S(2)}) %copy-start.2) | copy-done | bytes 152
  3.0 50.4 %shard_map.55 = bf16[256,4096]{1,0:T(8,128)(2,1)S(1)} custom-call(bf16[256,4096]{1,0:T(8,128)(2,1)S(1)} %copy-done, bf16[256,4096]{1,0:T(8,128)(2,1)} %k_hbm.1, bf16[256,4096]{1,0:T(8,128)(2,1)} %v_hbm.1, f32[32]{0:T(128)S(1)} %copy-done.2, f32[1,4096]{1,0:T(1,128)S(1)} %bitcast.1), custom_call_target="tpu_custom_call" | custom-call | flops 2147483648 | bytes 8388608 | tf_op jit(solution)/shard_map/pallas_call | solution.py:234
  53.3 1.3 %copy.7 = bf16[256,4096]{1,0:T(8,128)(2,1)} copy(bf16[256,4096]{1,0:T(8,128)(2,1)S(1)} %shard_map.55) | data formatting | bytes 4194304
Async XLA Ops:
  0.0 1.6 %copy-start = (bf16[256,4096]{1,0:T(8,128)(2,1)S(1)}, bf16[256,4096]{1,0:T(8,128)(2,1)}, u32[]{:S(2)}) copy-start(bf16[256,4096]{1,0:T(8,128)(2,1)} %q_hbm.1) | copy-start | bytes 6291460
  1.6 0.7 %copy-start.1 = (f32[4096]{0:T(1024)S(1)}, f32[4096]{0:T(1024)}, u32[]{:S(2)}) copy-start(f32[4096]{0:T(1024)} %param.9) | copy-start | bytes 49156
  2.3 0.7 %copy-start.2 = (f32[32]{0:T(128)S(1)}, f32[32]{0:T(128)}, u32[]{:S(2)}) copy-start(f32[32]{0:T(128)} %rates.1) | copy-start | bytes 388

commit v2 on v1

--- a/solution.py
+++ b/solution.py
@@ -9,8 +9,10 @@
 HEADS = 32
 HEAD_DIM = 128
 BLOCK = 256
-CHUNKS = 4
-PER_SLOT = 4
+CHUNKS = 8
+PER_SLOT = 2
+RATE_NEAR, RATE_FAR = 300e3, 50e3
+DELAY, INSIDE_COST = 1.6, 0.2
 F32 = jnp.float32
 BF16 = jnp.bfloat16
 
@@ -19,6 +21,40 @@
     high = x.astype(BF16)
     low = (x - high.astype(F32)).astype(BF16)
     return jnp.concatenate([high, low], axis=1)
+
+
+def plan(levels):
+    top = levels - 1
+    last = 2 * top + 1
+    rate = [RATE_NEAR] + [RATE_FAR] * top
+    volume = HEADS // CHUNKS * HEAD_DIM * HEAD_DIM * 4
+    step, ready = [0] * CHUNKS, [0.0] * CHUNKS
+    free = [0.0] * levels
+    now, inside_done, order = 0.0, 0, []
+    while min(step) <= last:
+        open_chunks = [c for c in range(CHUNKS) if step[c] <= last]
+        able = [c for c in open_chunks if ready[c] <= now]
+        early = [c for c in able if step[c] < last]
+        if not early and inside_done < HEADS:
+            order.append(("inside", inside_done))
+            inside_done += PER_SLOT
+            now += INSIDE_COST * PER_SLOT
+            continue
+        if not able:
+            now = min(ready[c] for c in open_chunks)
+            continue
+        c = max(early or able, key=lambda c: (step[c], -c))
+        e = step[c]
+        order.append((e, c))
+        now += (4.0 if e in (0, last) else 0.6) / CHUNKS + 0.1
+        step[c] += 1
+        if e < last:
+            k = e if e <= top else 2 * top - e
+            sent = volume >> (top if e == top else k + 1)
+            begin = max(now, free[k])
+            free[k] = begin + sent / rate[k]
+            ready[c] = free[k] + DELAY
+    return order
 
 
 def kernel(
@@ -98,7 +134,7 @@
             )
             return 0
 
-        lax.fori_loop(0, heads, one, 0, unroll=2)
+        lax.fori_loop(0, heads, one, 0, unroll=4)
 
     def segments(k, c):
         half = rows >> (k + 1)
@@ -149,7 +185,7 @@
             total[:, cols] = jnp.dot(weights, v_ref[:, cols], preferred_element_type=F32)
             return 0
 
-        lax.fori_loop(0, count, one, 0, unroll=2)
+        lax.fori_loop(0, count, one, 0, unroll=PER_SLOT)
 
     def finish(c):
         def one(i, _):
@@ -165,7 +201,7 @@
             o_ref[:, cols] = normed.astype(BF16)
             return 0
 
-        lax.fori_loop(0, heads, one, 0, unroll=2)
+        lax.fori_loop(0, heads, one, 0, unroll=4)
 
     top = levels - 1
 
@@ -196,21 +232,13 @@
                 finish(c)
                 save(c).start()
 
-    last = 2 * top + 1
-    done = 0
-    for slot in range(last + CHUNKS):
-        for c in range(CHUNKS):
-            if 0 <= slot - c <= last:
-                if slot - c == last:
-                    while done < (c + 1) * heads:
-                        inside(done, PER_SLOT)
-                        done += PER_SLOT
-                event(slot - c, c)
-        if slot >= 1 and done < HEADS:
-            if done % heads == 0:
-                load(2, done // heads).wait()
-            inside(done, PER_SLOT)
-            done += PER_SLOT
+    for e, c in plan(levels):
+        if e == "inside":
+            if c % heads == 0:
+                load(2, c // heads).wait()
+            inside(c, PER_SLOT)
+        else:
+            event(e, c)
     for c in range(CHUNKS):
         for k in range(levels):
             up_copy(k, c).wait_send()
@@ -256,7 +284,7 @@
             pltpu.SemaphoreType.DMA((top, CHUNKS)),
         ],
         compiler_params=pltpu.CompilerParams(
-            collective_id=0, has_side_effects=True, vmem_limit_bytes=48 << 20
+            collective_id=0, has_side_effects=True, vmem_limit_bytes=62 << 20
         ),
         cost_estimate=pl.CostEstimate(flops=2 << 30, bytes_accessed=8 << 20, transcendentals=4 << 20),
     )(queries, key_rows, value_rows, decay_rates, norm_gain.reshape(1, HEADS * HEAD_DIM))

time: 54.9 us -> 47.5 us (0.87)
  Pallas kernels: 50.4 us -> 44.2 us
  local copies, waits for them, and re-layouts: 4.28 us -> 3.13 us
    pallas_call x1, Pallas kernels: 50.4 us -> 44.2 us  [body(): pl.pallas_call(functools.partial(kernel, levels, minor), out_shape=jax.Sh...]
    unnamed x7 -> x1, local copies, waits for them, and re-layouts: 4.28 us -> 3.13 us
where the time goes in v2:
time: 47.5 us; the launch traced here: 47.3 us
  Pallas kernels  44.2 us (93%)
  local copies, waits for them, and re-layouts  3.13 us (7%)
    pallas_call x1, Pallas kernels, body(): pl.pallas_call(functools.partial(kernel, levels, minor), out_shape=jax.Sh...  44.2 us
    unnamed x1, local copies, waits for them, and re-layouts  3.13 us

profile of v2, /device:TPU:1, one launch (start us, length us, event | category | flops | bytes accessed | tf_op | source)
XLA Modules:
  0.0 47.3 jit_solution(14318434372645628950)
XLA Ops:
  0.0 44.2 %shard_map.55 = bf16[256,4096]{1,0:T(8,128)(2,1)} custom-call(bf16[256,4096]{1,0:T(8,128)(2,1)} %q_hbm.1, bf16[256,4096]{1,0:T(8,128)(2,1)} %k_hbm.1, bf16[256,4096]{1,0:T(8,128)(2,1)} %v_hbm.1, f32[32]{0:T(128)} %rates.1, f32[1,4096]{1,0:T(1,128)} %bitcast.1), custom_call_target="tpu_custom_call" | custom-call | flops 2147483648 | bytes 8388608 | tf_op jit(solution)/shard_map/pallas_call | solution.py:262
  44.2 3.1 %copy.7 = bf16[256,4096]{1,0:T(8,128)(2,1)} copy(bf16[256,4096]{1,0:T(8,128)(2,1)} %shard_map.55) | data formatting | bytes 4194304
